TPU v7x, 128 devices: a whole 4x4x4 slice. The times are simulated.
128 devices in a mesh: dp: 2 (over y_lo), sp: 64 (over z, y_hi, x, core).
Axes of the slice: x: 4, y: 4 (y_hi: 2, y_lo: 2; y = y_hi * 2 + y_lo), z: 4, core: 2. Of those that a mesh axis runs over, the one named last changes fastest.
Arguments:
- acts: bfloat16 [6, 12288, 384], P(None, ('dp', 'sp')), may hold values from -6 to 6
- cotangent: bfloat16 [6, 12288, 384], P(None, ('dp', 'sp')), may hold values from -24 to 24
- lengths: int32 [6, 16], replicated, may hold values from 672 to 768
- w_qkv: bfloat16 [2, 384, 1152], P(None, ('dp', 'sp')), may hold values from -0.3125 to 0.3125
- w_out: bfloat16 [2, 384, 384], P(None, ('dp', 'sp')), may hold values from -6 to 6
- w_up: bfloat16 [2, 384, 1536], P(None, ('dp', 'sp')), may hold values from -0.3125 to 0.3125
- w_down: bfloat16 [2, 384, 1536], P(None, ('dp', 'sp')), may hold values from -0.15625 to 0.15625
- gains: bfloat16 [2, 384, 2], P(None, ('dp', 'sp')), may hold values from 0.099609375 to 1.8984375
- biases: bfloat16 [2, 384, 6], P(None, ('dp', 'sp')), may hold values from -3 to 3
- hidden_bias: bfloat16 [2, 1536], P(None, 'dp'), may hold values from -3 to 3
Outputs:
- activations: float32 [6, 12288, 384], P(None, ('dp', 'sp'))
- input_grad: float32 [6, 12288, 384], P(None, ('dp', 'sp'))
- grad_w_qkv: float32 [2, 384, 1152], P(None, ('dp', 'sp'))
- grad_w_out: float32 [2, 384, 384], P(None, ('dp', 'sp'))
- grad_w_up: float32 [2, 384, 1536], P(None, ('dp', 'sp'))
- grad_w_down: float32 [2, 384, 1536], P(None, ('dp', 'sp'))
- grad_gains: float32 [2, 384, 2], P(None, ('dp', 'sp'))
- grad_biases: float32 [2, 384, 6], P(None, ('dp', 'sp'))
- grad_hidden_bias: float32 [2, 1536], P(None, 'dp')
Inputs may be any that keep to these rules, and one draw needn't show every extreme that they name: `lengths`: an image's valid tokens are its first ones; its other rows are padding.
All inputs are finite; a program needn't handle non-finite values.
Results may differ from a plain program's by a relative error of at most 0.011.
Values may be sent and summed in bfloat16 or wider, within the bound.
A program may use at most 256 MiB of HBM per device.

v0:
```python
import math

import jax
import jax.numpy as jnp
from jax import lax
from jax.sharding import PartitionSpec as P

HEADS = 6
HEAD_DIM = 64
LAYERS = 2
SPAN = 8


EPSILON = 1e-06
NEG_FILL = -1e30
GELU_COEF = math.sqrt(2.0 / math.pi)
CUBIC_COEF = 0.044715


def swapped(block, axis, apart):
    count = lax.axis_size(axis)
    route = []
    for low in range(count):
        high = low | 1 << apart
        if high != low and high < count:
            route += [(low, high), (high, low)]
    return lax.ppermute(block, axis, route)


def as_float(values):
    return values.astype(jnp.float32)


def product(left_side, right_side):
    return jnp.dot(left_side, right_side, preferred_element_type=jnp.float32)


def product_tn(left_side, right_side):
    return lax.dot_general(
        left_side, right_side, (((0,), (0,)), ((), ())), preferred_element_type=jnp.float32
    )


def product_nt(left_side, right_side):
    return lax.dot_general(
        left_side, right_side, (((1,), (1,)), ((), ())), preferred_element_type=jnp.float32
    )


def normalize(values):
    center = values - jnp.mean(values, axis=-1, keepdims=True)
    spread = jnp.mean(center * center, axis=-1, keepdims=True)
    inverse = lax.rsqrt(spread + EPSILON)
    return (center * inverse, inverse)


def norm_backward(upstream, normed, inverse, gain_vec):
    scaled = upstream * gain_vec
    centered = scaled - jnp.mean(scaled, axis=-1, keepdims=True)
    return inverse * (centered - normed * jnp.mean(scaled * normed, axis=-1, keepdims=True))


def gelu_pair(hidden):
    inner_arg = GELU_COEF * (hidden + CUBIC_COEF * hidden * hidden * hidden)
    tangent = jnp.tanh(inner_arg)
    gelu_value = 0.5 * hidden * (1.0 + tangent)
    gelu_slope = 0.5 * (1.0 + tangent) + 0.5 * hidden * (1.0 - tangent * tangent) * GELU_COEF * (
        1.0 + 3.0 * CUBIC_COEF * hidden * hidden
    )
    return (gelu_value, gelu_slope)


def fetch_layer(w_qkv, w_out, w_up, w_down, gains, biases, layer_index):
    return (
        lax.all_gather(w_qkv[layer_index], ("dp", "sp"), axis=0, tiled=True),
        lax.all_gather(w_out[layer_index], ("dp", "sp"), axis=0, tiled=True),
        lax.all_gather(w_up[layer_index], ("dp", "sp"), axis=0, tiled=True),
        lax.all_gather(w_down[layer_index], ("dp", "sp"), axis=0, tiled=True),
        lax.all_gather(gains[layer_index], ("dp", "sp"), axis=0, tiled=True),
        lax.all_gather(biases[layer_index], ("dp", "sp"), axis=0, tiled=True),
    )


def collect_image(key_part, value_part, position):
    for bit_number in range(SPAN.bit_length() - 1):
        other_key, other_value = swapped((key_part, value_part), "sp", bit_number)
        upper_half = position >> bit_number & 1 == 1
        key_part = jnp.where(
            upper_half,
            jnp.concatenate([other_key, key_part], 1),
            jnp.concatenate([key_part, other_key], 1),
        )
        value_part = jnp.where(
            upper_half,
            jnp.concatenate([other_value, value_part], 1),
            jnp.concatenate([value_part, other_value], 1),
        )
    return (key_part, value_part)


def reduce_image(key_grad, value_grad, position):
    for bit_number in reversed(range(SPAN.bit_length() - 1)):
        half_rows = key_grad.shape[1] // 2
        upper_half = position >> bit_number & 1 == 1
        keep_key = jnp.where(upper_half, key_grad[:, half_rows:], key_grad[:, :half_rows])
        send_key = jnp.where(upper_half, key_grad[:, :half_rows], key_grad[:, half_rows:])
        keep_value = jnp.where(upper_half, value_grad[:, half_rows:], value_grad[:, :half_rows])
        send_value = jnp.where(upper_half, value_grad[:, :half_rows], value_grad[:, half_rows:])
        got_key, got_value = (
            swapped(send_key.astype(jnp.bfloat16), "sp", bit_number).astype(send_key.dtype),
            swapped(send_value.astype(jnp.bfloat16), "sp", bit_number).astype(send_value.dtype),
        )
        key_grad = keep_key + got_key
        value_grad = keep_value + got_value
    return (key_grad, value_grad)


def local(acts, cotangent, lengths, w_qkv, w_out, w_up, w_down, gains, biases, hidden_bias):
    micro_count, piece_rows, features = acts.shape
    row_count = micro_count * piece_rows
    image_rows = SPAN * piece_rows
    score_scale = HEAD_DIM ** (-0.5)
    position = lax.axis_index("sp") % SPAN
    group_index = (lax.axis_index("dp") * lax.axis_size("sp") + lax.axis_index("sp")) // SPAN
    image_len = lax.dynamic_slice_in_dim(lengths, group_index, 1, 1)[:, 0]
    key_valid = jnp.arange(image_rows, dtype=jnp.int32)[None, :] < image_len[:, None]
    key_mask = key_valid[:, None, None, :]
    hidden_all = as_float(lax.all_gather(hidden_bias, "dp", axis=1, tiled=True))
    residual = as_float(acts).reshape(row_count, features)
    saved_layers = []
    for layer_index in range(LAYERS):
        fetched = fetch_layer(w_qkv, w_out, w_up, w_down, gains, biases, layer_index)
        mat_qkv, mat_out, mat_up, mat_down, gain_raw, shift_raw = fetched
        gain_cols = as_float(gain_raw)
        shift_cols = as_float(shift_raw)
        normed_one, inverse_one = normalize(residual)
        input_one = (normed_one * gain_cols[:, 0] + shift_cols[:, 3]).astype(jnp.bfloat16)
        qkv_bias = jnp.concatenate(
            [shift_cols[:, 0], jnp.zeros((features,), jnp.float32), shift_cols[:, 1]]
        )
        mixed_qkv = (product(input_one, mat_qkv) + qkv_bias).astype(jnp.bfloat16)
        queries = mixed_qkv[:, :features].reshape(micro_count, piece_rows, HEADS, HEAD_DIM)
        key_full, value_full = collect_image(
            mixed_qkv[:, features : 2 * features].reshape(micro_count, piece_rows, features),
            mixed_qkv[:, 2 * features :].reshape(micro_count, piece_rows, features),
            position,
        )
        key_heads = key_full.reshape(micro_count, image_rows, HEADS, HEAD_DIM)
        value_heads = value_full.reshape(micro_count, image_rows, HEADS, HEAD_DIM)
        scores = (
            jnp.einsum("mqhd,mkhd->mhqk", queries, key_heads, preferred_element_type=jnp.float32)
            * score_scale
        )
        scores = jnp.where(key_mask, scores, NEG_FILL)
        row_max = jnp.max(scores, axis=-1, keepdims=True)
        exponent = jnp.exp(scores - row_max)
        row_total = jnp.sum(exponent, axis=-1, keepdims=True)
        log_total = row_max + jnp.log(row_total)
        probabilities = (exponent / row_total).astype(jnp.bfloat16)
        attended = jnp.einsum(
            "mhqk,mkhd->mqhd", probabilities, value_heads, preferred_element_type=jnp.float32
        )
        attended = attended.reshape(row_count, features).astype(jnp.bfloat16)
        residual = residual + (product(attended, mat_out) + shift_cols[:, 2])
        normed_two, inverse_two = normalize(residual)
        input_two = (normed_two * gain_cols[:, 1] + shift_cols[:, 4]).astype(jnp.bfloat16)
        hidden = product(input_two, mat_up) + hidden_all[layer_index]
        active, gelu_slope = gelu_pair(hidden)
        active_low = active.astype(jnp.bfloat16)
        residual = residual + (product_nt(active_low, mat_down) + shift_cols[:, 5])
        kept_weights = None
        saved_layers.append(
            (
                normed_one,
                inverse_one,
                input_one,
                queries,
                key_heads,
                value_heads,
                log_total,
                attended,
                normed_two,
                inverse_two,
                input_two,
                gelu_slope,
                active_low,
                kept_weights,
            )
        )
    activations = residual.reshape(micro_count, piece_rows, features)
    carry = as_float(cotangent).reshape(row_count, features)
    layer_grads = [None] * LAYERS
    hidden_grads = [None] * LAYERS
    for layer_index in reversed(range(LAYERS)):
        (
            normed_one,
            inverse_one,
            input_one,
            queries,
            key_heads,
            value_heads,
            log_total,
            attended,
            normed_two,
            inverse_two,
            input_two,
            gelu_slope,
            active_low,
            kept_weights,
        ) = saved_layers[layer_index]
        fetched = fetch_layer(w_qkv, w_out, w_up, w_down, gains, biases, layer_index)
        mat_qkv, mat_out, mat_up, mat_down, gain_raw, shift_raw = fetched
        gain_cols = as_float(gain_raw)
        down_grad = carry.astype(jnp.bfloat16)
        grad_down_bias = jnp.sum(as_float(down_grad), axis=0)
        grad_mat_down = product_tn(down_grad, active_low)
        hidden_grad = (product(down_grad, mat_down) * gelu_slope).astype(jnp.bfloat16)
        hidden_grads[layer_index] = jnp.sum(as_float(hidden_grad), axis=0)
        grad_mat_up = product_tn(input_two, hidden_grad)
        input_two_grad = product_nt(hidden_grad, mat_up)
        grad_gain_two = jnp.sum(input_two_grad * normed_two, axis=0)
        grad_shift_two = jnp.sum(input_two_grad, axis=0)
        carry = carry + norm_backward(input_two_grad, normed_two, inverse_two, gain_cols[:, 1])
        out_grad = carry.astype(jnp.bfloat16)
        grad_out_bias = jnp.sum(as_float(out_grad), axis=0)
        grad_mat_out = product_tn(attended, out_grad)
        attended_grad = (
            product_nt(out_grad, mat_out)
            .astype(jnp.bfloat16)
            .reshape(micro_count, piece_rows, HEADS, HEAD_DIM)
        )
        scores = (
            jnp.einsum("mqhd,mkhd->mhqk", queries, key_heads, preferred_element_type=jnp.float32)
            * score_scale
        )
        scores = jnp.where(key_mask, scores, NEG_FILL)
        probs_full = jnp.exp(scores - log_total)
        probs_low = probs_full.astype(jnp.bfloat16)
        prob_grad = jnp.einsum(
            "mqhd,mkhd->mhqk", attended_grad, value_heads, preferred_element_type=jnp.float32
        )
        score_grad = (
            probs_full * (prob_grad - jnp.sum(probs_full * prob_grad, axis=-1, keepdims=True))
        ).astype(jnp.bfloat16)
        query_grad = (
            jnp.einsum("mhqk,mkhd->mqhd", score_grad, key_heads, preferred_element_type=jnp.float32)
            * score_scale
        )
        key_part = (
            jnp.einsum("mhqk,mqhd->mkhd", score_grad, queries, preferred_element_type=jnp.float32)
            * score_scale
        )
        value_part = jnp.einsum(
            "mhqk,mqhd->mkhd", probs_low, attended_grad, preferred_element_type=jnp.float32
        )
        key_grad, value_grad = reduce_image(
            key_part.reshape(micro_count, image_rows, features),
            value_part.reshape(micro_count, image_rows, features),
            position,
        )
        mixed_grad = jnp.concatenate(
            [
                query_grad.reshape(row_count, features),
                key_grad.reshape(row_count, features),
                value_grad.reshape(row_count, features),
            ],
            1,
        ).astype(jnp.bfloat16)
        grad_query_bias = jnp.sum(as_float(mixed_grad[:, :features]), axis=0)
        grad_value_bias = jnp.sum(as_float(mixed_grad[:, 2 * features :]), axis=0)
        grad_mat_qkv = product_tn(input_one, mixed_grad)
        input_one_grad = product_nt(mixed_grad, mat_qkv)
        grad_gain_one = jnp.sum(input_one_grad * normed_one, axis=0)
        grad_shift_one = jnp.sum(input_one_grad, axis=0)
        carry = carry + norm_backward(input_one_grad, normed_one, inverse_one, gain_cols[:, 0])
        gain_grads = jnp.stack([grad_gain_one, grad_gain_two], 1)
        shift_grads = jnp.stack(
            [
                grad_query_bias,
                grad_value_bias,
                grad_out_bias,
                grad_shift_one,
                grad_shift_two,
                grad_down_bias,
            ],
            1,
        )
        layer_grads[layer_index] = (
            lax.psum_scatter(grad_mat_qkv, ("dp", "sp"), scatter_dimension=0, tiled=True),
            lax.psum_scatter(grad_mat_out, ("dp", "sp"), scatter_dimension=0, tiled=True),
            lax.psum_scatter(grad_mat_up, ("dp", "sp"), scatter_dimension=0, tiled=True),
            lax.psum_scatter(grad_mat_down, ("dp", "sp"), scatter_dimension=0, tiled=True),
            lax.psum_scatter(gain_grads, ("dp", "sp"), scatter_dimension=0, tiled=True),
            lax.psum_scatter(shift_grads, ("dp", "sp"), scatter_dimension=0, tiled=True),
        )
    hidden_total = lax.psum(jnp.stack(hidden_grads, 0), ("dp", "sp"))
    shard_width = hidden_bias.shape[1]
    hidden_share = lax.dynamic_slice_in_dim(
        hidden_total, lax.axis_index("dp") * shard_width, shard_width, 1
    )
    stacked = [
        jnp.stack([layer_grads[layer_index][member] for layer_index in range(LAYERS)], 0)
        for member in range(6)
    ]
    input_grad = carry.reshape(micro_count, piece_rows, features)
    return (
        activations,
        input_grad,
        stacked[0],
        stacked[1],
        stacked[2],
        stacked[3],
        stacked[4],
        stacked[5],
        hidden_share,
    )


def solution(mesh):
    in_specs = (
        P(None, ("dp", "sp"), None),
        P(None, ("dp", "sp"), None),
        P(),
        P(None, ("dp", "sp"), None),
        P(None, ("dp", "sp"), None),
        P(None, ("dp", "sp"), None),
        P(None, ("dp", "sp"), None),
        P(None, ("dp", "sp"), None),
        P(None, ("dp", "sp"), None),
        P(None, "dp"),
    )
    out_specs = (
        P(None, ("dp", "sp"), None),
        P(None, ("dp", "sp"), None),
        P(None, ("dp", "sp"), None),
        P(None, ("dp", "sp"), None),
        P(None, ("dp", "sp"), None),
        P(None, ("dp", "sp"), None),
        P(None, ("dp", "sp"), None),
        P(None, ("dp", "sp"), None),
        P(None, "dp"),
    )
    return jax.shard_map(local, mesh=mesh, in_specs=in_specs, out_specs=out_specs, check_vma=False)
```

profile of v0, /device:TPU:1, one launch (start us, length us, event | category | flops | bytes accessed | tf_op | source)
XLA Modules:
  0.0 2362.7 jit_solution(5807165886397302801)
XLA Ops:
  14.5 180.6 %all-gather.7 = bf16[1,384,6]{2,0,1:T(2,128)(2,1)S(1)} all-gather(bf16[1,3,6]{2,0,1:T(2,128)(2,1)S(1)} %get-tuple-element.122), channel_id=9, replica_groups=mesh['dp'=2,'sp'=64] {'dp','sp'}, dimensions={1}, use_global_device_ids=true | all-gather | bytes 4644 | tf_op jit(solution)/shard_map/all_gather | solution.py:80
  196.5 170.9 %all-gather = bf16[1,384,2]{2,0,1:T(2,128)(2,1)S(1)} all-gather(bf16[1,3,2]{2,0,1:T(2,128)(2,1)S(1)} %copy.269), channel_id=2, replica_groups=mesh['dp'=2,'sp'=64] {'dp','sp'}, dimensions={1}, use_global_device_ids=true | all-gather | bytes 1548 | tf_op jit(solution)/shard_map/all_gather | solution.py:79
  367.9 172.3 %all-gather.1 = bf16[1,384,6]{2,0,1:T(2,128)(2,1)S(1)} all-gather(bf16[1,3,6]{2,0,1:T(2,128)(2,1)S(1)} %get-tuple-element.123), channel_id=3, replica_groups=mesh['dp'=2,'sp'=64] {'dp','sp'}, dimensions={1}, use_global_device_ids=true | all-gather | bytes 4644 | tf_op jit(solution)/shard_map/all_gather | solution.py:80
  542.6 175.2 %all-gather.2 = bf16[1,384,1152]{2,0,1:T(2,128)(2,1)S(1)} all-gather(bf16[1,3,1152]{2,0,1:T(2,128)(2,1)S(1)} %get-tuple-element.117), channel_id=4, replica_groups=mesh['dp'=2,'sp'=64] {'dp','sp'}, dimensions={1}, use_global_device_ids=true | all-gather | bytes 891648 | tf_op jit(solution)/shard_map/all_gather | solution.py:75
  724.3 184.3 %all-gather.6 = bf16[1,384,2]{2,0,1:T(2,128)(2,1)S(1)} all-gather(bf16[1,3,2]{2,0,1:T(2,128)(2,1)S(1)} %copy.270), channel_id=8, replica_groups=mesh['dp'=2,'sp'=64] {'dp','sp'}, dimensions={1}, use_global_device_ids=true | all-gather | bytes 1548 | tf_op jit(solution)/shard_map/all_gather | solution.py:79
  910.8 194.2 %all-gather.3 = bf16[1,384,384]{2,0,1:T(2,128)(2,1)} all-gather(bf16[1,3,384]{2,0,1:T(2,128)(2,1)S(1)} %get-tuple-element.119), channel_id=5, replica_groups=mesh['dp'=2,'sp'=64] {'dp','sp'}, dimensions={1}, use_global_device_ids=true | all-gather | bytes 297216 | tf_op jit(solution)/shard_map/all_gather | solution.py:76
  1126.8 242.7 %all-gather.8 = bf16[1,384,1152]{2,0,1:T(2,128)(2,1)} all-gather(bf16[1,3,1152]{2,0,1:T(2,128)(2,1)S(1)} %get-tuple-element.116), channel_id=10, replica_groups=mesh['dp'=2,'sp'=64] {'dp','sp'}, dimensions={1}, use_global_device_ids=true | all-gather | bytes 891648 | tf_op jit(solution)/shard_map/all_gather | solution.py:75
  1371.4 6.5 maximum_select_fusion.12
  1382.8 5.2 maximum_select_fusion.4
  1395.8 8.0 maximum_select_fusion.1
  1408.0 4.4 maximum_select_fusion
  1419.4 4.7 fusion.72
  1426.0 4.7 convolution_add_fusion.3
  1430.7 4.4 fusion.156
  1443.2 17.6 collective-permute-done.10
  1462.5 18.0 collective-permute-done.7
  1484.2 246.4 %all-gather.9 = bf16[1,384,384]{2,0,1:T(2,128)(2,1)} all-gather(bf16[1,3,384]{2,0,1:T(2,128)(2,1)} %get-tuple-element.118), channel_id=11, replica_groups=mesh['dp'=2,'sp'=64] {'dp','sp'}, dimensions={1}, use_global_device_ids=true | all-gather | bytes 297216 | tf_op jit(solution)/shard_map/all_gather | solution.py:76
  1745.6 4.6 maximum_select_fusion.15
  1758.3 5.3 maximum_select_fusion.6
  1771.4 7.9 maximum_select_fusion.3
  1783.6 4.4 maximum_select_fusion.2
  1794.9 4.5 fusion.75
  1801.4 4.6 convolution_add_fusion.2
  1806.0 6.0 convert_reduce_fusion
  1819.7 11.0 multiply_reduce_fusion.1
  1830.7 5.0 fusion.6
  1849.4 5.2 copy.272
  1856.5 6.4 fusion.146
  1862.9 5.2 copy.273
  1868.1 5.2 copy.274
  1886.7 5.6 fusion.69
  1903.7 32.6 %collective-permute-done.15 = bf16[6,384,384]{2,1,0:T(8,128)(2,1)} collective-permute-done((bf16[6,384,384]{2,1,0:T(8,128)(2,1)}, bf16[6,384,384]{2,1,0:T(8,128)(2,1)}, u32[]{:S(2)}, u32[]{:S(2)}) %collective-permute-start.15) | collective-permute-done | bytes 1769504 | tf_op jit(solution)/shard_map/ppermute | solution.py:27
  1943.0 11.1 collective-permute-done.13
  1955.4 17.6 collective-permute-done.16
  1999.2 11.4 multiply_reduce_fusion
  2020.5 8.4 multiply_convert_fusion
  2034.9 5.2 copy.275
  2040.1 5.4 copy.276
  2052.7 5.2 copy.278
  2061.8 5.6 fusion.66
  2071.1 4.5 fusion.141
  2078.7 13.3 collective-permute-done.18
  2094.6 35.3 %collective-permute-done.21 = bf16[6,384,384]{2,1,0:T(8,128)(2,1)} collective-permute-done((bf16[6,384,384]{2,1,0:T(8,128)(2,1)}, bf16[6,384,384]{2,1,0:T(8,128)(2,1)}, u32[]{:S(2)}, u32[]{:S(2)}) %collective-permute-start.21) | collective-permute-done | bytes 1769504 | tf_op jit(solution)/shard_map/ppermute | solution.py:27
  2134.9 12.9 collective-permute-done.19
  2149.4 17.4 collective-permute-done.22
  2178.9 5.8 fusion.65
  2189.0 65.6 %all-reduce.12 = (f32[384,2]{0,1:T(2,128)S(1)}, f32[384,2]{0,1:T(2,128)S(1)}, f32[384,6]{0,1:T(8,128)S(1)}, f32[384,6]{0,1:T(8,128)S(1)}, f32[2,1536]{1,0:T(2,128)S(1)}) all-reduce(f32[384,2]{0,1:T(2,128)S(1)} %pad_maximum_fusion.15, f32[384,2]{0,1:T(2,128)S(1)} %pad_maximum_fusion.14, ...), channel_id=23, replica_groups=mesh['dp'=2,'sp'=64] {'dp','sp'}, use_global_device_ids=true, to_apply=%region_35.36.clone | all-reduce | flops 9216 | bytes 73728
  2258.2 88.1 %all-reduce.16.cloned.1.call-done = (f32[384,1152]{1,0:T(8,128)}, f32[384,1152]{1,0:T(8,128)}, f32[384,384]{1,0:T(8,128)}, f32[384,384]{1,0:T(8,128)}, f32[384,1...) async-done(((f32[384,1152]{1,0:T(8,128)}, f32[384,1152]{1,0:T(8,128)}, f32[384,384]{1,0:T(8,128)}, f32[384,384]{1,0:T(8,128)}, ...) | async-done | bytes 14155792
  (558 shorter events, 279.8 us)
Async XLA Ops:
  7.2 1105.1 %copy-start = (s32[6,16]{1,0:T(8,128)S(1)}, s32[6,16]{1,0:T(8,128)}, u32[]{:S(2)}) copy-start(s32[6,16]{1,0:T(8,128)} %param.12) | copy-start | bytes 1156
  7.2 534.4 %copy-start.18 = (bf16[6,96,384]{2,1,0:T(8,128)(2,1)S(1)}, bf16[6,96,384]{2,1,0:T(8,128)(2,1)}, u32[]{:S(2)}) copy-start(bf16[6,96,384]{2,1,0:T(8,128)(2,1)} %param.10) | copy-start | bytes 1327108
  7.2 535.3 %copy-start.74 = (bf16[2,3,1152]{2,0,1:T(2,128)(2,1)S(1)}, bf16[2,3,1152]{2,0,1:T(2,128)(2,1)}, u32[]{:S(2)}) copy-start(bf16[2,3,1152]{2,0,1:T(2,128)(2,1)} %param.13) | copy-start | bytes 41476
  7.2 1418.8 %all-gather.17.cloned.1.call-start = ((), (), s32[]{:S(2)}) async-start(), calls=%async_computation | async-start | bytes 2377728 | tf_op jit(solution)/shard_map/all_gather | solution.py:77
  8.7 1422.0 %all-gather.19.cloned.1.call-start = ((), (), s32[]{:S(2)}) async-start(), calls=%async_computation.1 | async-start | bytes 2377728 | tf_op jit(solution)/shard_map/all_gather | solution.py:78
  10.3 1791.1 %all-gather.21.cloned.1.call-start = ((), (), s32[]{:S(2)}) async-start(), calls=%async_computation.2 | async-start | bytes 2377728 | tf_op jit(solution)/shard_map/all_gather | solution.py:77
  11.6 706.2 %copy-start.75 = (f32[576]{0:T(1024)}, f32[576]{0:T(1024)S(1)}, u32[]{:S(2)}) copy-start(f32[576]{0:T(1024)S(1)} %div.75) | copy-start | bytes 6916
  14.5 703.2 %copy-start.77 = (f32[576]{0:T(1024)}, f32[576]{0:T(1024)S(1)}, u32[]{:S(2)}) copy-start(f32[576]{0:T(1024)S(1)} %rsqrt.36) | copy-start | bytes 6916
  367.9 349.9 %copy-start.82 = (f32[384]{0:T(512)}, f32[384]{0:T(512)S(1)}, u32[]{:S(2)}) copy-start(f32[384]{0:T(512)S(1)} %get-tuple-element.70) | copy-start | bytes 4612
  367.9 1058.1 %copy-start.92 = (f32[384]{0:T(512)}, f32[384]{0:T(512)S(1)}, u32[]{:S(2)}) copy-start(f32[384]{0:T(512)S(1)} %get-tuple-element.69) | copy-start | bytes 4612
  541.8 177.8 %copy-start.66 = (bf16[576,384]{1,0:T(8,128)(2,1)}, bf16[576,384]{1,0:T(8,128)(2,1)S(1)}, u32[]{:S(2)}) copy-start(bf16[576,384]{1,0:T(8,128)(2,1)S(1)} %add_convert_fusion.7) | copy-start | bytes 1327108
  718.7 191.5 %copy-start.81 = (bf16[2,3,384]{2,0,1:T(2,128)(2,1)S(1)}, bf16[2,3,384]{2,0,1:T(2,128)(2,1)}, u32[]{:S(2)}) copy-start(bf16[2,3,384]{2,0,1:T(2,128)(2,1)} %param.14) | copy-start | bytes 13828
  719.6 1.8 collective-permute-start.3
  719.8 189.0 %collective-permute-start = (bf16[6,96,384]{2,1,0:T(8,128)(2,1)S(1)}, bf16[6,96,384]{2,1,0:T(8,128)(2,1)S(1)}, u32[]{:S(2)}, u32[]{:S(2)}) collective-permute-start(bf16[6,96,384]{2,1,0:T(8,128)(2,1)S(1)} %bitcast.214), channel_id=1, source_target_pairs={{0,1},{1,0},{2,3},{3,2},{4,5},{5,4},{6,7},{7,6},{8,9},{9,8},{10,11... | collective-permute-start | bytes 1327112 | tf_op jit(solution)/shard_map/ppermute | solution.py:27
  722.7 386.4 %copy-start.110 = (bf16[2,768]{1,0:T(2,128)(2,1)S(1)}, bf16[2,768]{1,0:T(2,128)(2,1)}, u32[]{:S(2)}) copy-start(bf16[2,768]{1,0:T(2,128)(2,1)} %param.19) | copy-start | bytes 9220
  722.7 382.3 %collective-permute-start.4 = (bf16[6,192,384]{2,1,0:T(8,128)(2,1)}, bf16[6,192,384]{2,1,0:T(8,128)(2,1)S(1)}, u32[]{:S(2)}, u32[]{:S(2)}) collective-permute-start(bf16[6,192,384]{2,1,0:T(8,128)(2,1)} %maximum_select_fusion.17), channel_id=1, source_target_pairs={{0,2},{2,0},{1,3},{3,1},{4,6},{6,4},{5,7},{7,5},{8,10},{10,8},{9,1... | collective-permute-start | bytes 2654216 | tf_op jit(solution)/shard_map/ppermute | solution.py:27
  724.1 1081.9 %all-gather.23.cloned.1.call-start = ((), (), s32[]{:S(2)}) async-start(), calls=%async_computation.3 | async-start | bytes 2377728 | tf_op jit(solution)/shard_map/all_gather | solution.py:78
  908.8 207.5 %copy-start.57 = (bf16[6,96,384]{2,1,0:T(8,128)(2,1)}, bf16[6,96,384]{2,1,0:T(8,128)(2,1)S(1)}, u32[]{:S(2)}) copy-start(bf16[6,96,384]{2,1,0:T(8,128)(2,1)S(1)} %collective-permute-done) | copy-start | bytes 1327108
  910.1 202.4 %collective-permute-start.1 = (bf16[6,192,384]{2,1,0:T(8,128)(2,1)}, bf16[6,192,384]{2,1,0:T(8,128)(2,1)}, u32[]{:S(2)}, u32[]{:S(2)}) collective-permute-start(bf16[6,192,384]{2,1,0:T(8,128)(2,1)} %maximum_select_fusion.16), channel_id=1, source_target_pairs={{0,2},{2,0},{1,3},{3,1},{4,6},{6,4},{5,7},{7,5},{8,10},{10,8},{9,1... | collective-permute-start | bytes 2654216 | tf_op jit(solution)/shard_map/ppermute | solution.py:27
  1108.3 283.3 %collective-permute-start.5 = (bf16[6,384,384]{2,1,0:T(8,128)(2,1)}, bf16[6,384,384]{2,1,0:T(8,128)(2,1)}, u32[]{:S(2)}, u32[]{:S(2)}) collective-permute-start(bf16[6,384,384]{2,1,0:T(8,128)(2,1)} %maximum_select_fusion.9), channel_id=1, source_target_pairs={{0,4},{4,0},{1,5},{5,1},{2,6},{6,2},{3,7},{7,3},{8,12},{12,8},{9,1... | collective-permute-start | bytes 5308424 | tf_op jit(solution)/shard_map/ppermute | solution.py:27
  1116.4 287.4 %collective-permute-start.2 = (bf16[6,384,384]{2,1,0:T(8,128)(2,1)}, bf16[6,384,384]{2,1,0:T(8,128)(2,1)}, u32[]{:S(2)}, u32[]{:S(2)}) collective-permute-start(bf16[6,384,384]{2,1,0:T(8,128)(2,1)} %maximum_select_fusion.8), channel_id=1, source_target_pairs={{0,4},{4,0},{1,5},{5,1},{2,6},{6,2},{3,7},{7,3},{8,12},{12,8},{9,1... | collective-permute-start | bytes 5308424 | tf_op jit(solution)/shard_map/ppermute | solution.py:27
  1122.3 247.2 %copy-start.56 = (bf16[6,96,384]{2,1,0:T(8,128)(2,1)S(1)}, bf16[6,96,384]{2,1,0:T(8,128)(2,1)}, u32[]{:S(2)}) copy-start(bf16[6,96,384]{2,1,0:T(8,128)(2,1)} %copy-done.55) | copy-start | bytes 1327108
  1122.3 247.7 %copy-start.58 = (bf16[6,96,384]{2,1,0:T(8,128)(2,1)S(1)}, bf16[6,96,384]{2,1,0:T(8,128)(2,1)}, u32[]{:S(2)}) copy-start(bf16[6,96,384]{2,1,0:T(8,128)(2,1)} %copy-done.57) | copy-start | bytes 1327108
  1436.6 1.9 collective-permute-start.9
  1436.9 2.8 collective-permute-start.6
  1439.6 21.2 collective-permute-start.10
  1441.8 288.8 %copy-start.39 = (bf16[6,96,384]{2,1,0:T(8,128)(2,1)S(1)}, bf16[6,96,384]{2,1,0:T(8,128)(2,1)}, u32[]{:S(2)}) copy-start(bf16[6,96,384]{2,1,0:T(8,128)(2,1)} %param.11) | copy-start | bytes 1327108
  1441.8 38.8 %collective-permute-start.7 = (bf16[6,192,384]{2,1,0:T(8,128)(2,1)}, bf16[6,192,384]{2,1,0:T(8,128)(2,1)S(1)}, u32[]{:S(2)}, u32[]{:S(2)}) collective-permute-start(bf16[6,192,384]{2,1,0:T(8,128)(2,1)} %maximum_select_fusion.18), channel_id=1, source_target_pairs={{0,2},{2,0},{1,3},{3,1},{4,6},{6,4},{5,7},{7,5},{8,10},{10,8},{9,1... | collective-permute-start | bytes 2654216 | tf_op jit(solution)/shard_map/ppermute | solution.py:27
  1462.5 304.7 %collective-permute-start.11 = (bf16[6,384,384]{2,1,0:T(8,128)(2,1)}, bf16[6,384,384]{2,1,0:T(8,128)(2,1)}, u32[]{:S(2)}, u32[]{:S(2)}) collective-permute-start(bf16[6,384,384]{2,1,0:T(8,128)(2,1)} %maximum_select_fusion.11), channel_id=1, source_target_pairs={{0,4},{4,0},{1,5},{5,1},{2,6},{6,2},{3,7},{7,3},{8,12},{12,8},{9,1... | collective-permute-start | bytes 5308424 | tf_op jit(solution)/shard_map/ppermute | solution.py:27
  1462.5 883.8 %all-reduce.16.cloned.1.call-start = ((), (), s32[]{:S(2)}) async-start(), calls=%async_computation.4 | async-start | bytes 28311552
  1480.5 255.8 %copy-start.45 = (bf16[6,192,384]{2,1,0:T(8,128)(2,1)}, bf16[6,192,384]{2,1,0:T(8,128)(2,1)S(1)}, u32[]{:S(2)}) copy-start(bf16[6,192,384]{2,1,0:T(8,128)(2,1)S(1)} %collective-permute-done.7) | copy-start | bytes 2654212
  1484.2 295.1 %collective-permute-start.8 = (bf16[6,384,384]{2,1,0:T(8,128)(2,1)}, bf16[6,384,384]{2,1,0:T(8,128)(2,1)}, u32[]{:S(2)}, u32[]{:S(2)}) collective-permute-start(bf16[6,384,384]{2,1,0:T(8,128)(2,1)} %maximum_select_fusion.10), channel_id=1, source_target_pairs={{0,4},{4,0},{1,5},{5,1},{2,6},{6,2},{3,7},{7,3},{8,12},{12,8},{9,1... | collective-permute-start | bytes 5308424 | tf_op jit(solution)/shard_map/ppermute | solution.py:27
  1856.5 41.9 %collective-permute-start.12 = (bf16[6,384,384]{2,1,0:T(8,128)(2,1)}, bf16[6,384,384]{2,1,0:T(8,128)(2,1)}, u32[]{:S(2)}, u32[]{:S(2)}) collective-permute-start(bf16[6,384,384]{2,1,0:T(8,128)(2,1)} %select_convert_fusion.3), channel_id=1, source_target_pairs={{0,4},{4,0},{1,5},{5,1},{2,6},{6,2},{3,7},{7,3},{8,12},{12,8},{9,1... | collective-permute-start | bytes 5308424 | tf_op jit(solution)/shard_map/ppermute | solution.py:27
  1877.0 59.3 %collective-permute-start.15 = (bf16[6,384,384]{2,1,0:T(8,128)(2,1)}, bf16[6,384,384]{2,1,0:T(8,128)(2,1)}, u32[]{:S(2)}, u32[]{:S(2)}) collective-permute-start(bf16[6,384,384]{2,1,0:T(8,128)(2,1)} %select_convert_fusion.2), channel_id=1, source_target_pairs={{0,4},{4,0},{1,5},{5,1},{2,6},{6,2},{3,7},{7,3},{8,12},{12,8},{9,1... | collective-permute-start | bytes 5308424 | tf_op jit(solution)/shard_map/ppermute | solution.py:27
  1902.0 38.2 %copy-start.27 = (f32[576,384]{1,0:T(8,128)S(1)}, f32[576,384]{1,0:T(8,128)}, u32[]{:S(2)}) copy-start(f32[576,384]{1,0:T(8,128)} %copy-done.26) | copy-start | bytes 2654212
  1902.0 38.2 %copy-start.85 = (f32[576]{0:T(1024)S(1)}, f32[576]{0:T(1024)}, u32[]{:S(2)}) copy-start(f32[576]{0:T(1024)} %copy-done.84) | copy-start | bytes 6916
  1902.0 38.2 %copy-start.99 = (f32[384]{0:T(512)S(1)}, f32[384]{0:T(512)}, u32[]{:S(2)}) copy-start(f32[384]{0:T(512)} %get-tuple-element.61) | copy-start | bytes 4612
  1902.1 52.0 %collective-permute-start.13 = (bf16[6,192,384]{2,1,0:T(8,128)(2,1)S(1)}, bf16[6,192,384]{2,1,0:T(8,128)(2,1)S(1)}, u32[]{:S(2)}, u32[]{:S(2)}) collective-permute-start(bf16[6,192,384]{2,1,0:T(8,128)(2,1)S(1)} %select_convert_fusion.7), channel_id=1, source_target_pairs={{0,2},{2,0},{1,3},{3,1},{4,6},{6,4},{5,7},{7,5},{8,10},{10,8},{9,1... | collective-permute-start | bytes 2654216 | tf_op jit(solution)/shard_map/ppermute | solution.py:27
  1938.6 34.4 %collective-permute-start.16 = (bf16[6,192,384]{2,1,0:T(8,128)(2,1)S(1)}, bf16[6,192,384]{2,1,0:T(8,128)(2,1)S(1)}, u32[]{:S(2)}, u32[]{:S(2)}) collective-permute-start(bf16[6,192,384]{2,1,0:T(8,128)(2,1)S(1)} %select_convert_fusion.6), channel_id=1, source_target_pairs={{0,2},{2,0},{1,3},{3,1},{4,6},{6,4},{5,7},{7,5},{8,10},{10,8},{9,1... | collective-permute-start | bytes 2654216 | tf_op jit(solution)/shard_map/ppermute | solution.py:27
  1954.4 21.7 collective-permute-start.14
  1974.2 4.9 collective-permute-start.17
  2049.1 42.9 %collective-permute-start.18 = (bf16[6,384,384]{2,1,0:T(8,128)(2,1)}, bf16[6,384,384]{2,1,0:T(8,128)(2,1)}, u32[]{:S(2)}, u32[]{:S(2)}) collective-permute-start(bf16[6,384,384]{2,1,0:T(8,128)(2,1)} %select_convert_fusion.1), channel_id=1, source_target_pairs={{0,4},{4,0},{1,5},{5,1},{2,6},{6,2},{3,7},{7,3},{8,12},{12,8},{9,1... | collective-permute-start | bytes 5308424 | tf_op jit(solution)/shard_map/ppermute | solution.py:27
  2059.8 70.2 %collective-permute-start.21 = (bf16[6,384,384]{2,1,0:T(8,128)(2,1)}, bf16[6,384,384]{2,1,0:T(8,128)(2,1)}, u32[]{:S(2)}, u32[]{:S(2)}) collective-permute-start(bf16[6,384,384]{2,1,0:T(8,128)(2,1)} %select_convert_fusion), channel_id=1, source_target_pairs={{0,4},{4,0},{1,5},{5,1},{2,6},{6,2},{3,7},{7,3},{8,12},{12,8},{9,1... | collective-permute-start | bytes 5308424 | tf_op jit(solution)/shard_map/ppermute | solution.py:27
  2094.5 53.3 %collective-permute-start.19 = (bf16[6,192,384]{2,1,0:T(8,128)(2,1)S(1)}, bf16[6,192,384]{2,1,0:T(8,128)(2,1)S(1)}, u32[]{:S(2)}, u32[]{:S(2)}) collective-permute-start(bf16[6,192,384]{2,1,0:T(8,128)(2,1)S(1)} %select_convert_fusion.5), channel_id=1, source_target_pairs={{0,2},{2,0},{1,3},{3,1},{4,6},{6,4},{5,7},{7,5},{8,10},{10,8},{9,1... | collective-permute-start | bytes 2654216 | tf_op jit(solution)/shard_map/ppermute | solution.py:27
  2132.3 34.5 %collective-permute-start.22 = (bf16[6,192,384]{2,1,0:T(8,128)(2,1)S(1)}, bf16[6,192,384]{2,1,0:T(8,128)(2,1)S(1)}, u32[]{:S(2)}, u32[]{:S(2)}) collective-permute-start(bf16[6,192,384]{2,1,0:T(8,128)(2,1)S(1)} %select_convert_fusion.4), channel_id=1, source_target_pairs={{0,2},{2,0},{1,3},{3,1},{4,6},{6,4},{5,7},{7,5},{8,10},{10,8},{9,1... | collective-permute-start | bytes 2654216 | tf_op jit(solution)/shard_map/ppermute | solution.py:27
  2148.2 22.0 collective-permute-start.20
  2167.9 3.4 collective-permute-start.23
  2185.4 170.4 %copy-start.1 = (s32[6,16]{1,0:T(8,128)S(1)}, s32[6,16]{1,0:T(8,128)}, u32[]{:S(2)}) copy-start(s32[6,16]{1,0:T(8,128)} %param.12) | copy-start | bytes 1156
  (123 other events, 1133.4 us)
Sparse Core Ops, SparseCore 0:
  9.8 198.9 all-gather.16
  210.5 194.5 all-gather.18
  724.2 190.8 all-gather.20
  1462.6 263.2 all-gather.22
  2176.5 169.7 all-reduce.15
where the time goes:
time: 2370 us; the launch traced here: 2360 us
  blocking collectives  1640 us (69%)
  waiting for transfers between devices  269 us (11%)
  local copies, waits for them, and re-layouts  161 us (7%)
  other arithmetic  133 us (6%)
  matrix products  125 us (5%)
    all_gather x2, blocking collectives, fetch_layer(): lax.all_gather(w_out[layer_index], ('dp', 'sp'), axis=0, tiled=True)  441 us
    all_gather x2, blocking collectives, fetch_layer(): lax.all_gather(w_qkv[layer_index], ('dp', 'sp'), axis=0, tiled=True)  418 us
    all_gather x2, blocking collectives, fetch_layer(): lax.all_gather(gains[layer_index], ('dp', 'sp'), axis=0, tiled=True)  355 us
    all_gather x2, blocking collectives, fetch_layer(): lax.all_gather(biases[layer_index], ('dp', 'sp'), axis=0, tiled=True)  353 us
    ppermute x24, waiting for transfers between devices, swapped(): return lax.ppermute(block, axis, route)  181 us
    unnamed x6, waiting for transfers between devices  88.2 us
    unnamed x1, blocking collectives  65.6 us
    unnamed x301, local copies, waits for them, and re-layouts  53.5 us
  transfers between devices with their start and end apart: 29, of which 13 were waited for; matrix products, arithmetic and copies ran while one was open for 12% of the time, Pallas kernels for 0%

commit v1 on v0

v1 whole, which is shorter than its diff:
```python
import math

import jax
import jax.numpy as jnp
from jax import lax
from jax.experimental import pallas as pl
from jax.experimental.pallas import tpu as pltpu
from jax.sharding import PartitionSpec as P

D = 384
HEADS = 6
PAIRS = HEADS // 2
HEAD_DIM = 64
FF = 1536
LAYERS = 2
TOK = 768
EPSILON = 1e-06
NEG_FILL = -1e30
GELU_COEF = math.sqrt(2.0 / math.pi)
CUBIC_COEF = 0.044715
BF = jnp.bfloat16
F32 = jnp.float32
RB = 384
FC = 512
MIB = 1024 * 1024

MISC0, OUT0, UP0, DOWN0, WIDE = 1152, 1280, 1664, 3200, 4864
UNITS = (
    (0, 0, 640, 384, (0, 32)),
    (0, 1280, 896, 384, (32, 64)),
    (0, 3072, 896, 384, (64, 96)),
    (1, 0, 640, 384, (0, 32)),
    (1, 1280, 1792, 896, (32, 96)),
)
COUNT = len(UNITS)
SLAB = 96
GROUPS = ((0, 0, 32), (0, 32, 96), (1, 0, 96))

OWNERS = (0, 1, 2, 4, 5, 6)
MESH = pl.DeviceIdType.MESH
SPLIT = 16
ROWS = 48


def dot(left_side, right_side):
    return jnp.dot(left_side, right_side, preferred_element_type=F32)


def dot_nt(left_side, right_side):
    return lax.dot_general(
        left_side, right_side, (((1,), (1,)), ((), ())), preferred_element_type=F32
    )


def dot_tn(left_side, right_side):
    return lax.dot_general(
        left_side, right_side, (((0,), (0,)), ((), ())), preferred_element_type=F32
    )


def normalized(values):
    center = values - jnp.mean(values, axis=-1, keepdims=True)
    inverse = lax.rsqrt(jnp.mean(center * center, axis=-1, keepdims=True) + EPSILON)
    return center * inverse, inverse


def norm_backward(upstream, xhat, inverse, gain):
    scaled = upstream * gain
    return inverse * (
        scaled
        - jnp.mean(scaled, axis=-1, keepdims=True)
        - xhat * jnp.mean(scaled * xhat, axis=-1, keepdims=True)
    )


def gelu_pair(hidden):
    square = hidden * hidden
    tangent = jnp.tanh(hidden * (GELU_COEF + (GELU_COEF * CUBIC_COEF) * square))
    half = 0.5 + 0.5 * tangent
    active = hidden * half
    slope = half + active * (1.0 - tangent) * (
        GELU_COEF + (3.0 * GELU_COEF * CUBIC_COEF) * square
    )
    return active, slope


def colsum(values):
    return jnp.sum(values.astype(F32), axis=0, keepdims=True)


def each_block(body):
    for start in range(0, TOK, RB):
        body(slice(start, start + RB))


def each_chunk(stop, width, body):
    for start in range(0, stop, width):
        body(slice(start, start + width), lambda base, at=start: slice(base + at, base + at + width))


def encoder(
    length, w, carry, inputs, cot, act, igrad, hid, hid_sums, row_sums,
    mids, qkv, probs_even, probs_odd, invs, att, att_low, active, slope, low_a, low_b, dqkv, trans, trans_b, prm,
):
    last_valid = lax.broadcasted_iota(jnp.int32, (1, 128), 1) + (TOK - 128) < length
    lanes = lax.broadcasted_iota(jnp.int32, (1, 128), 1)
    first_half = lanes < 64
    scale = HEAD_DIM ** (-0.5)

    def lanes_at(pair, base):
        return pl.ds(pl.multiple_of(base + 128 * pair, 128), 128)

    def half_of(block, which):
        keep = first_half if which == 0 else jnp.logical_not(first_half)
        return jnp.where(keep, block, jnp.zeros_like(block))

    def row(layer, index):
        at = (index + 6) % 8
        return prm[layer, at : at + 1, :]

    def project(layer):
        prm[layer] = w[layer, :, MISC0 : MISC0 + 128].astype(F32).T[0:8]

        bias = jnp.concatenate([row(layer, 2), jnp.zeros((1, D), F32), row(layer, 3)], axis=1)

        def body(rows):
            source = carry[rows, :]
            inputs[layer, rows, :] = source
            xhat, _inverse = normalized(source)
            low = (xhat * row(layer, 0) + row(layer, 5)).astype(BF)
            qkv[layer, rows, :] = (dot(low, w[layer, :, 0 : 3 * D]) + bias).astype(BF)

        each_block(body)
        trans[...] = qkv[layer, :, D : 2 * D].T

    def attend(layer, pair):
        lane = lanes_at(pair, 0)
        value = qkv[layer, :, lanes_at(pair, 2 * D)]
        value = jnp.concatenate([value, jnp.ones((TOK, 128), BF)], axis=1)

        def body(rows):
            query = qkv[layer, rows, lane] * jnp.asarray(scale, BF)
            results = []
            kept = invs[rows, :]
            for which in range(2):
                head = 2 * pair + which
                scores = dot(half_of(query, which), trans[lane, :])
                last = jnp.where(last_valid, scores[:, TOK - 128 :], NEG_FILL)
                scores = jnp.concatenate([scores[:, : TOK - 128], last], axis=1)
                low = jnp.exp(scores - jnp.max(scores, axis=-1, keepdims=True)).astype(BF)
                (probs_even, probs_odd)[which][layer, pair, rows, :] = low
                product = dot(low, value)
                inverse = 1.0 / product[:, 128:]
                results.append(product[:, :128] * inverse)
                kept = jnp.where(lanes == 8 * layer + head, inverse, kept)
            invs[rows, :] = kept
            whole = jnp.where(first_half, results[0], results[1])
            high = whole.astype(BF)
            att[layer, rows, lane] = high
            att_low[layer, rows, lane] = (whole - high.astype(F32)).astype(BF)

        each_block(body)

    def feed(layer):
        def body(rows):
            mid = inputs[layer, rows, :] + (
                dot(att[layer, rows, :], w[layer, :, OUT0 : OUT0 + D]) + row(layer, 4)
            )
            mids[layer, rows, :] = mid
            xhat, _inverse = normalized(mid)
            low = (xhat * row(layer, 1) + row(layer, 6)).astype(BF)
            total = mid + row(layer, 7)
            for chunk in range(FF // FC):
                cols = slice(FC * chunk, FC * chunk + FC)
                hidden = dot(low, w[layer, :, UP0 + FC * chunk : UP0 + FC * chunk + FC])
                value, rate = gelu_pair(hidden + hid[layer, :, cols])
                value = value.astype(BF)
                active[layer, rows, cols] = value
                slope[layer, rows, cols] = rate.astype(BF)
                total = total + dot_nt(
                    value, w[layer, :, DOWN0 + FC * chunk : DOWN0 + FC * chunk + FC]
                )
            carry[rows, :] = total
            act[rows, :] = total.astype(BF)

        each_block(body)

    def add_sum(layer, index, values):
        row_sums[layer, index : index + 1, :] += colsum(values)

    def turn_back():
        carry[...] = cot[...].astype(F32)

    def unfeed(layer):
        def body(rows):
            upstream = carry[rows, :]
            down = upstream.astype(BF)
            low_a[rows, :] = down
            add_sum(layer, 7, down)
            xhat, inverse = normalized(mids[layer, rows, :])
            low_b[rows, :] = (xhat * row(layer, 1) + row(layer, 6)).astype(BF)
            total = jnp.zeros((RB, D), F32)
            for chunk in range(FF // FC):
                cols = slice(FC * chunk, FC * chunk + FC)
                grad = dot(down, w[layer, :, DOWN0 + FC * chunk : DOWN0 + FC * chunk + FC])
                grad = (grad * slope[layer, rows, cols].astype(F32)).astype(BF)
                slope[layer, rows, cols] = grad
                hid_sums[layer, chunk : chunk + 1, :] += colsum(grad)
                total = total + dot_nt(grad, w[layer, :, UP0 + FC * chunk : UP0 + FC * chunk + FC])
            add_sum(layer, 1, total * xhat)
            add_sum(layer, 6, total)
            carry[rows, :] = upstream + norm_backward(total, xhat, inverse, row(layer, 1))

        each_block(body)

    def feed_grads(layer):
        trans[...] = low_a[...].T
        trans_b[...] = low_b[...].T

        def grad_down(cols, at):
            w[layer, :, at(DOWN0)] = dot(trans[...], active[layer, :, cols]).astype(BF)

        def grad_up(cols, at):
            w[layer, :, at(UP0)] = dot(trans_b[...], slope[layer, :, cols]).astype(BF)

        each_chunk(FF, FC, grad_down)
        each_chunk(FF, FC, grad_up)

    def unproject_out(layer):
        def body(rows):
            low = carry[rows, :].astype(BF)
            low_a[rows, :] = low
            add_sum(layer, 4, low)
            grad = dot_nt(low, w[layer, :, OUT0 : OUT0 + D])
            inverse = jnp.where(layer == 0, invs[rows, 0:8], invs[rows, 8:16])
            for pair in range(PAIRS):
                lane = slice(128 * pair, 128 * pair + 128)
                both = jnp.where(
                    first_half,
                    inverse[:, 2 * pair : 2 * pair + 1],
                    inverse[:, 2 * pair + 1 : 2 * pair + 2],
                )
                low_b[rows, lane] = (grad[:, lane] * both).astype(BF)

        each_block(body)
        trans[...] = att[layer].T
        w[layer, :, OUT0 : OUT0 + D] = dot(trans[...], low_a[...]).astype(BF)
        trans[...] = low_b[...].T
        trans_b[...] = (qkv[layer, :, 0:D] * jnp.asarray(scale, BF)).T

    def unattend(layer, pair):
        lane = lanes_at(pair, 0)
        key = qkv[layer, :, lanes_at(pair, D)]
        value = qkv[layer, :, lanes_at(pair, 2 * D)]
        key_parts, value_parts = [0.0, 0.0], [0.0, 0.0]

        def body(rows):
            grad = low_b[rows, lane]
            whole = att[layer, rows, lane].astype(F32) + att_low[layer, rows, lane].astype(F32)
            weighted = grad.astype(F32) * whole
            results = []
            for which, probs in enumerate((probs_even, probs_odd)):
                feature = pl.ds(pl.multiple_of(128 * pair + 64 * which, 64), 64)
                low = probs[layer, pair, rows, :]
                inner = jnp.sum(half_of(weighted, which), axis=-1, keepdims=True)
                prob_grad = dot_nt(half_of(grad, which), value)
                score_grad = (low.astype(F32) * (prob_grad - inner)).astype(BF)
                results.append(dot(score_grad, key))
                key_parts[which] += dot(trans_b[feature, rows], score_grad)
                value_parts[which] += dot(trans[feature, rows], low)
            dqkv[rows, lane] = (jnp.where(first_half, results[0], results[1]) * scale).astype(BF)

        each_block(body)
        dqkv[:, lanes_at(pair, D)] = jnp.concatenate(key_parts, axis=0).T.astype(BF)
        dqkv[:, lanes_at(pair, 2 * D)] = jnp.concatenate(value_parts, axis=0).T.astype(BF)

    def qkv_grads(layer):
        def body(rows):
            xhat, _inverse = normalized(inputs[layer, rows, :])
            low_a[rows, :] = (xhat * row(layer, 0) + row(layer, 5)).astype(BF)

        each_block(body)
        trans[...] = low_a[...].T

        def grad_qkv(cols, _at):
            active[layer, 0:D, cols] = dot(trans[...], dqkv[:, cols]).astype(BF)

        each_chunk(3 * D, D, grad_qkv)

    def unproject(layer, between):
        def body(rows):
            if rows.stop == TOK:
                between()
            add_sum(layer, 2, dqkv[rows, 0:D])
            add_sum(layer, 3, dqkv[rows, 2 * D : 3 * D])
            xhat, inverse = normalized(inputs[layer, rows, :])
            total = dot_nt(dqkv[rows, :], w[layer, :, 0 : 3 * D])
            add_sum(layer, 0, total * xhat)
            add_sum(layer, 5, total)
            upstream = carry[rows, :] + norm_backward(total, xhat, inverse, row(layer, 0))
            carry[rows, :] = upstream
            igrad[rows, :] = upstream.astype(BF)

        each_block(body)

    return (
        project, attend, feed, turn_back, unfeed, feed_grads, unproject_out, unattend, qkv_grads, unproject,
    )


def compute_scratch():
    return [
        pltpu.VMEM((LAYERS, TOK, D), F32),
        pltpu.VMEM((LAYERS, TOK, 3 * D), BF),
        pltpu.VMEM((LAYERS, PAIRS, TOK, TOK), BF),
        pltpu.VMEM((LAYERS, PAIRS, TOK, TOK), BF),
        pltpu.VMEM((TOK, 128), F32),
        pltpu.VMEM((LAYERS, TOK, D), BF),
        pltpu.VMEM((LAYERS, TOK, D), BF),
        pltpu.VMEM((LAYERS, TOK, FF), BF),
        pltpu.VMEM((LAYERS, TOK, FF), BF),
        pltpu.VMEM((TOK, D), BF),
        pltpu.VMEM((TOK, 3 * D), BF),
        pltpu.VMEM((D, TOK), BF),
        pltpu.VMEM((D, TOK), BF),
        pltpu.VMEM((LAYERS, 8, D), F32),
    ]


def device(dp, z, y, x, core):
    return (dp, z * 16 + y * 8 + x * 2 + core)


def turned(value, by, count):
    return lax.rem(value + (by + count), count)


def rows_at(block):
    return pl.ds(pl.multiple_of(block * ROWS, 16), ROWS)


def image_rows(position):
    return pl.ds(pl.multiple_of(position * 96, 16), 96)


def copy_to(source, target, send, recv, where):
    return pltpu.make_async_remote_copy(
        src_ref=source,
        dst_ref=target,
        send_sem=send,
        recv_sem=recv,
        device_id=where,
        device_id_type=MESH,
    )


def spread_matrix():
    out = lax.broadcasted_iota(jnp.int32, (4 * ROWS, 256), 0)
    col = lax.broadcasted_iota(jnp.int32, (4 * ROWS, 256), 1)
    member, inner, row = col >> 4, (col >> 2) & 3, col & 3
    hit = jnp.logical_and(out == ROWS * inner + 3 * member + row, row < 3)
    return jnp.where(hit, 1.0, 0.0).astype(BF)


def kernel(
    lengths, acts, cot_in, p_qkv, p_out, p_up, p_down, p_gains, p_biases, p_hid,
    o_qkv, o_out, o_up, o_down, o_gains, o_biases, o_hid, act_out, igrad_out,
    w, carry, inputs, img, cot, act, onehot, slab_build, hid_all, hid, hid_sums, row_sums, early, late, tall_sums,
    mids, qkv, probs_even, probs_odd, invs, att, att_low, active, slope, low_b, dqkv, trans, trans_b, prm,
    give, held, slabs, ends,
    h_core, h_y, h_z, h_p, h_sum, l_plane, l_far, l_sum,
    ga_send, ga_recv, gz_send, gz_recv, gy_send, gy_recv, gs_send, gs_recv,
    i_send, i_recv, i_local, b_send, b_recv,
    rc_send, rc_recv, ry_send, ry_recv, rz_send, rz_recv, rp_send, rp_recv,
    e_send, e_recv, e_local, h_send, h_recv, l_send, l_recv,
    *buffers,
):
    core_buf, y_buf, z_buf = [buffers[COUNT * kind : COUNT * kind + COUNT] for kind in range(3)]
    dp, sp = lax.axis_index("dp"), lax.axis_index("sp")
    z = lax.div(sp, 16)
    y = lax.rem(lax.div(sp, 8), 2)
    x = lax.rem(lax.div(sp, 2), 4)
    core = lax.rem(sp, 2)
    mine = y * 8 + x * 2 + core
    position = x * 2 + core
    entry_mine = position - lax.div(position, 4)
    owner = lax.rem(position, 4) < 3
    sibling = device(dp, z, y, x, 1 - core)
    igrad = img
    low_a = cot
    gathers, reduces = [], []

    def push(source, target, send, recv, where):
        copy_to(source, target, send, recv, where).start()

    def all_sent(steps):
        for view, sem, index in steps:
            ref, sem = view(), sem.at[index]
            copy_to(ref, ref, sem, sem, sibling).wait_send()

    def sent(steps, view, sem, *index):
        steps.append((view, sem, index))

    def arrived(ref, send, recv):
        copy_to(ref, ref, send, recv, sibling).wait_recv()

    peers = [sibling]
    for step in range(1, 4):
        peers.append(device(dp, z, y, turned(x, step, 4), core))
        peers.append(device(dp, z, y, turned(x, step, 4), 1 - core))
        peers.append(device(dp, turned(z, step, 4), y, x, core))
        peers.append(device(1 - dp, turned(z, step, 4), y, x, core))
    for step in range(4):
        peers.append(device(dp, z, 1 - y, turned(x, step, 4), core))
        peers.append(device(dp, z, 1 - y, turned(x, step, 4), 1 - core))
    for side in (y, 1 - y):
        peers.append(device(1 - dp, z, side, x, core))
    barrier = pltpu.get_barrier_semaphore()
    for peer in peers:
        pl.semaphore_signal(barrier, inc=1, device_id=peer, device_id_type=MESH)

    def misc_rows(layer):
        slab_build[0:8, :] = jnp.zeros((8, 128), F32)
        slab_build[0:3, 0:6] = p_biases[...].astype(F32)[:, layer, :]
        rows = slab_build[0:3, :]
        at = lax.broadcasted_iota(jnp.int32, (3, 128), 0)
        lane = lax.broadcasted_iota(jnp.int32, (3, 128), 1)
        gains = p_gains[...].astype(F32)
        for gain in range(2):
            for feature in range(3):
                hit = jnp.logical_and(at == feature, lane == 6 + gain)
                rows = jnp.where(hit, gains[layer, gain : gain + 1, feature : feature + 1], rows)
        return rows

    def slab_build_layer(layer):
        whole = jnp.concatenate(
            [p_qkv[...].astype(F32)[:, layer, :], misc_rows(layer)]
            + [ref[...].astype(F32)[:, layer, :] for ref in (p_out, p_up, p_down)]
            + [jnp.zeros((3, 128), F32)],
            axis=1,
        )
        for side in range(2):
            slab_build[...] = jnp.zeros_like(slab_build)
            for of, start, width, _first, rows in UNITS:
                for chunk in range(width // 128) if of == layer else ():
                    at = start + side * width + 128 * chunk
                    row = rows[0] + 4 * chunk
                    slab_build[row : row + 3, :] = whole[:, at : at + 128]
            give[layer, side] = slab_build[...].astype(BF)

    slab_build_layer(0)
    pl.semaphore_wait(barrier, len(peers))

    def plane_target(turn):
        return turned(y, turn // 8, 2), turned(x, turn // 2 % 4, 4), turned(core, turn % 2, 2)

    def plane_source(turn):
        return (
            turned(y, -(turn // 8), 2) * 8
            + turned(x, -(turn // 2 % 4), 4) * 2
            + turned(core, -(turn % 2), 2)
        )

    def slab_send(group):
        layer, begin, end = GROUPS[group]
        held[layer, mine, begin:end, :] = give[layer, core, begin:end, :]
        for turn in range(1, 16):
            to_y, to_x, to_core = plane_target(turn)
            push(
                give.at[layer, to_core, begin:end, :],
                held.at[layer, mine, begin:end, :],
                ga_send.at[group],
                ga_recv.at[group],
                device(dp, z, to_y, to_x, to_core),
            )
        sent(gathers, lambda: held.at[layer, 1:16, begin:end, :], ga_send, group)

    def slab_arrive(group):
        layer, begin, end = GROUPS[group]
        arrived(held.at[layer, 1:16, begin:end, :], ga_send.at[group], ga_recv.at[group])

    def cols_of(unit, side, part):
        _layer, start, width, first, _rows = UNITS[unit]
        begin, count = ((0, width), (0, first), (first, width - first))[0 if part is None else part + 1]
        return pl.ds(pl.multiple_of(start + side * width + begin, 128), count)

    def unit_view(unit, rows, side, part=None):
        return w.at[UNITS[unit][0], rows, cols_of(unit, side, part)]

    def rows_of(side):
        return pl.ds(pl.multiple_of(side * (4 * ROWS), 16), 4 * ROWS)

    def block_build(unit):
        layer, start, width, _first, (begin, end) = UNITS[unit]
        block = rows_at(dp * 4 + z)
        for group in range((end - begin) // 16):
            at = begin + 16 * group
            tall = held[layer, :, at : at + 16, :].reshape(256, 128)
            wide = dot(onehot[...], tall).astype(BF)
            for inner in range(4):
                chunk = 4 * group + inner
                if chunk < width // 128:
                    cols = pl.ds(pl.multiple_of(start + core * width + 128 * chunk, 128), 128)
                    w[layer, block, cols] = wide[ROWS * inner : ROWS * inner + ROWS]
        ref = unit_view(unit, block, core)
        turns = range(1, 8 if unit == 0 else 4)
        for turn in turns:
            where = device(turned(dp, turn // 4, 2), turned(z, turn % 4, 4), y, x, core)
            push(ref, ref, gz_send.at[unit], gz_recv.at[unit], where)
        sent(gathers, lambda: w.at[layer, 0 : len(turns) * ROWS, 0:width], gz_send, unit)

    def gather_direct(unit):
        layer, _start, width, _first, _rows = UNITS[unit]
        arrived(unit_view(unit, slice(0, 7 * ROWS), core), gz_send.at[unit], gz_recv.at[unit])
        ref = unit_view(unit, slice(0, D), core)
        push(ref, ref, gs_send.at[unit], gs_recv.at[unit], sibling)
        sent(gathers, lambda: w.at[layer, :, 0:width], gs_send, unit)

    def gather_z(unit):
        layer, _start, width, _first, _rows = UNITS[unit]
        arrived(unit_view(unit, slice(0, 3 * ROWS), core), gz_send.at[unit], gz_recv.at[unit])
        for part in range(2):
            ref = unit_view(unit, rows_of(dp), core, part)
            where = device(1 - dp, z, (y, 1 - y)[part], x, core)
            push(ref, ref, gy_send.at[unit], gy_recv.at[unit], where)
        sent(gathers, lambda: w.at[layer, 0 : 4 * ROWS, 0:width], gy_send, unit)
        ref = unit_view(unit, rows_of(dp), core)
        push(ref, ref, gs_send.at[unit], gs_recv.at[unit], sibling)

    def gather_y(unit):
        layer, _start, width, _first, _rows = UNITS[unit]
        ref = unit_view(unit, rows_of(1 - dp), core)
        arrived(ref, gy_send.at[unit], gy_recv.at[unit])
        push(ref, ref, gs_send.at[unit], gs_recv.at[unit], sibling)
        sent(gathers, lambda: w.at[layer, :, 0:width], gs_send, unit)

    def gather_end(unit):
        arrived(unit_view(unit, slice(0, D), 1 - core), gs_send.at[unit], gs_recv.at[unit])

    moves = ((acts, img), (cot_in, cot))

    def image_copy(index, entry, home):
        source, target = moves[index]
        return copy_to(
            source.at[entry],
            target.at[image_rows(position), :],
            i_send.at[index],
            i_recv.at[index],
            device(dp, z, y, home // 2, home % 2),
        )

    def image_local(index, entry):
        source, target = moves[index]
        return pltpu.make_async_copy(
            source.at[entry], target.at[image_rows(position), :], i_local.at[index]
        )

    def image_send(index):
        for entry, home in enumerate(OWNERS):

            @pl.when(position != home)
            def _():
                image_copy(index, entry, home).start()

            @pl.when(position == home)
            def _():
                image_local(index, entry).start()

    def image_arrive(index):
        source, target = moves[index]

        @pl.when(jnp.logical_not(owner))
        def _():
            target[...] = jnp.zeros_like(target)
            copy_to(source, source, i_send.at[index], i_recv.at[index], sibling).wait_send()

        @pl.when(owner)
        def _():
            image_local(index, 0).wait()
            ref = source.at[0:5]
            copy_to(ref, ref, i_send.at[index], i_recv.at[index], sibling).wait_send()
            arrived(target.at[0 : 7 * 96, :], i_send.at[index], i_recv.at[index])

    def grad_root(unit):
        return active if UNITS[unit][1] == 0 else w

    def grad_view(unit, rows, side, part=None):
        return grad_root(unit).at[UNITS[unit][0], rows, cols_of(unit, side, part)]

    def reduce_core(unit):
        layer, _start, width, _first, _rows = UNITS[unit]
        root = grad_root(unit)
        for index, side in enumerate((1 - dp, dp)):
            push(
                grad_view(unit, rows_of(side), 1 - core),
                core_buf[unit].at[index],
                rc_send.at[unit],
                rc_recv.at[unit, index],
                sibling,
            )
        sent(reduces, lambda: root.at[layer, 0:D, 0:width], rc_send, unit)

    def reduce_y(unit):
        layer, _start, width, first, _rows = UNITS[unit]
        arrived(core_buf[unit].at[0], rc_send.at[unit], rc_recv.at[unit, 0])

        def add(block, carried):
            ref = grad_view(unit, rows_at((1 - dp) * 4 + block), core)
            ref[...] = (ref[...].astype(F32) + core_buf[unit][0, rows_at(block), :].astype(F32)).astype(BF)
            return carried

        lax.fori_loop(0, 4, add, 0)
        for part, cols in enumerate((slice(0, first), slice(first, width))):
            push(
                grad_view(unit, rows_of(1 - dp), core, part),
                y_buf[unit].at[:, cols],
                ry_send.at[unit],
                ry_recv.at[unit],
                device(1 - dp, z, (y, 1 - y)[part], x, core),
            )
        sent(reduces, lambda: y_buf[unit], ry_send, unit)

    def reduce_z(unit):
        layer, _start, width, first, _rows = UNITS[unit]
        arrived(core_buf[unit].at[1], rc_send.at[unit], rc_recv.at[unit, 1])
        arrived(y_buf[unit], ry_send.at[unit], ry_recv.at[unit])
        for turn in (1, 2, 3, 0):
            block = turned(z, turn, 4)
            ref = grad_view(unit, rows_at(dp * 4 + block), core)
            total = (
                ref[...].astype(F32)
                + core_buf[unit][1, rows_at(block), :].astype(F32)
                + y_buf[unit][rows_at(block), :].astype(F32)
            )
            ref[...] = total.astype(BF)
            if turn:
                push(
                    ref,
                    z_buf[unit].at[turn - 1],
                    rz_send.at[unit],
                    rz_recv.at[unit],
                    device(dp, block, y, x, core),
                )
        sent(reduces, lambda: z_buf[unit], rz_send, unit)

    def reduce_direct(unit):
        layer, _start, width, _first, _rows = UNITS[unit]
        for index in range(2):
            arrived(core_buf[unit].at[index], rc_send.at[unit], rc_recv.at[unit, index])
        for turn in (1, 2, 3, 4, 5, 6, 7, 0):
            to_dp, to_z = turned(dp, turn // 4, 2), turned(z, turn % 4, 4)
            ref = grad_view(unit, rows_at(to_dp * 4 + to_z), core)
            total = ref[...].astype(F32) + core_buf[unit][1 - turn // 4, rows_at(to_z), :].astype(F32)
            ref[...] = total.astype(BF)
            if turn:
                push(
                    ref,
                    z_buf[unit].at[turn - 1],
                    rz_send.at[unit],
                    rz_recv.at[unit],
                    device(to_dp, to_z, y, x, core),
                )
        sent(reduces, lambda: z_buf[unit], rz_send, unit)

    def reduce_slab(unit):
        layer, _start, width, _first, (begin, end) = UNITS[unit]
        total = grad_view(unit, rows_at(dp * 4 + z), core)[...].astype(F32)
        arrived(z_buf[unit], rz_send.at[unit], rz_recv.at[unit])
        for turn in range(1, 8 if unit == 0 else 4):
            total = total + z_buf[unit][turn - 1].astype(F32)
        low = total.astype(BF)
        for group in range((end - begin) // 16):
            parts = [
                low[:, 128 * chunk : 128 * chunk + 128]
                if chunk < width // 128
                else jnp.zeros((ROWS, 128), BF)
                for chunk in range(4 * group, 4 * group + 4)
            ]
            tall = dot_tn(onehot[...], jnp.concatenate(parts, axis=0)).astype(BF)
            at = begin + 16 * group
            slabs[layer, :, at : at + 16, :] = tall.reshape(SPLIT, 16, 128)

    def reduce_plane(group):
        layer, begin, end = GROUPS[group]
        for turn in range(1, 16):
            to_y, to_x, to_core = plane_target(turn)
            push(
                slabs.at[layer, to_y * 8 + to_x * 2 + to_core, begin:end, :],
                ends.at[layer, turn, begin:end, :],
                rp_send.at[group],
                rp_recv.at[group],
                device(dp, z, to_y, to_x, to_core),
            )
        sent(reduces, lambda: slabs.at[layer, 1:16, begin:end, :], rp_send, group)

    outs = ((o_qkv, 0, 9), (o_out, 10, 13), (o_up, 13, 25), (o_down, 25, 37))

    def reduce_end(group):
        layer, begin, end = GROUPS[group]
        totals = [slabs[layer, mine, begin:end, :].astype(F32), None]
        arrived(ends.at[layer, 1:16, begin:end, :], rp_send.at[group], rp_recv.at[group])
        for turn in range(1, 16):
            value = ends[layer, turn, begin:end, :].astype(F32)
            side = turn % 2
            totals[side] = value if totals[side] is None else totals[side] + value
        first = core == 0
        halves = (
            jnp.where(first, totals[0], totals[1]),
            jnp.where(first, totals[1], totals[0]),
        )
        for of, start, width, _first, (low, high) in UNITS:
            for chunk in range(width // 64) if of == layer and begin <= low and high <= end else ():
                inner = low - begin + 4 * (chunk % (width // 128))
                rows = halves[chunk // (width // 128)][inner : inner + 3]
                for target, lowest, highest in outs:
                    if lowest <= start // 128 + chunk < highest:
                        at = 128 * (start // 128 + chunk - lowest)
                        target[:, layer, at : at + 128] = rows

    def misc_out(layer, total):
        tall_sums[...] = jnp.concatenate([total, jnp.zeros((120, D), F32)], axis=0).T
        at = lax.broadcasted_iota(jnp.int32, (8, 128), 0)
        rows = jnp.zeros((8, 128), F32)
        for feature in range(3):
            line = tall_sums[pl.ds(3 * (dp * 64 + sp) + feature, 1), :]
            o_biases[feature, layer : layer + 1, :] = line[:, 2:8]
            rows = jnp.where(at == feature, line, rows)
        wide = jnp.concatenate([rows, jnp.zeros((120, 128), F32)], axis=0).T
        o_gains[layer] = wide[0:2, 0:3]

    def early_sum(stage):
        def send(source, target, where):
            push(source, target, h_send.at[stage], h_recv.at[stage], where)

        def wait(ref):
            arrived(ref, h_send.at[stage - 1], h_recv.at[stage - 1])

        if stage == 0:
            for layer in range(LAYERS):
                early[3 * layer : 3 * layer + 3, :] = hid_sums[layer]
            early[8:16, 0:D] = row_sums[1]
            send(early, h_core, sibling)
            sent(reduces, lambda: early, h_send, 0)
        elif stage == 1:
            wait(h_core)
            h_sum[0] = early[...] + h_core[...]
            send(h_sum.at[0], h_y, device(1 - dp, z, y, x, core))
            sent(reduces, lambda: early, h_send, 1)
        elif stage == 2:
            wait(h_y)
            h_sum[1] = h_sum[0] + h_y[...]
            for turn in range(1, 4):
                send(h_sum.at[1], h_z.at[turn - 1], device(dp, turned(z, turn, 4), y, x, core))
            sent(reduces, lambda: h_z, h_send, 2)
        elif stage == 3:
            wait(h_z)
            h_sum[2] = h_sum[1] + h_z[0] + h_z[1] + h_z[2]
            for turn in range(1, 8):
                where = device(dp, z, turned(y, turn // 4, 2), turned(x, turn % 4, 4), core)
                send(h_sum.at[2], h_p.at[turn], where)
            sent(reduces, lambda: h_p.at[1:8], h_send, 3)
        else:
            wait(h_p.at[1:8])
            total = h_sum[2]
            for turn in range(1, 8):
                total = total + h_p[turn]
            for layer in range(LAYERS):
                for chunk in range(FF // FC):
                    hid[layer, :, FC * chunk : FC * chunk + FC] = total[
                        3 * layer + chunk : 3 * layer + chunk + 1
                    ]
            for layer in range(LAYERS):
                share = pl.ds(pl.multiple_of(dp * (FF // 2), 128), FF // 2)
                o_hid[layer : layer + 1, :] = hid[layer, :, share]
            misc_out(1, total[8:16, 0:D])

    def late_sum(stage):
        if stage == 0:
            late[...] = row_sums[0]
            for turn in range(1, 16):
                where = device(dp, z, *plane_target(turn))
                push(late, l_plane.at[turn], l_send.at[0], l_recv.at[0], where)
            sent(reduces, lambda: l_plane.at[1:16], l_send, 0)
        elif stage == 1:
            arrived(l_plane.at[1:16], l_send.at[0], l_recv.at[0])
            total = late[...]
            for turn in range(1, 16):
                total = total + l_plane[turn]
            l_sum[...] = total
            for turn in range(1, 8):
                where = device(turned(dp, turn // 4, 2), turned(z, turn % 4, 4), y, x, core)
                push(l_sum, l_far.at[turn], l_send.at[1], l_recv.at[1], where)
            sent(reduces, lambda: l_far.at[1:8], l_send, 1)
        else:
            arrived(l_far.at[1:8], l_send.at[1], l_recv.at[1])
            total = l_sum[...]
            for turn in range(1, 8):
                total = total + l_far[turn]
            misc_out(0, total)

    backs = ((act, act_out), (igrad, igrad_out))

    def back_copy(index, home):
        source, target = backs[index]
        return copy_to(
            source.at[96 * home : 96 * home + 96, :],
            target.at[entry_mine],
            e_send.at[index],
            e_recv.at[index],
            device(dp, z, y, home // 2, home % 2),
        )

    def back_local(index, home):
        source, target = backs[index]
        return pltpu.make_async_copy(
            source.at[96 * home : 96 * home + 96, :], target.at[entry_mine], e_local.at[index]
        )

    def back_send(index, first, last):
        for home in range(first, last):

            @pl.when(jnp.logical_and(owner, position != home))
            def _():
                back_copy(index, home).start()

            @pl.when(jnp.logical_and(owner, position == home))
            def _():
                back_local(index, home).start()

    def back_arrive(index):
        source, target = backs[index]

        @pl.when(owner)
        def _():
            back_local(index, 0).wait()
            ref = source.at[0 : 7 * 96, :]
            copy_to(ref, ref, e_send.at[index], e_recv.at[index], sibling).wait_send()
            arrived(target.at[0:5], e_send.at[index], e_recv.at[index])

        @pl.when(jnp.logical_not(owner))
        def _():
            arrived(target, e_send.at[index], e_recv.at[index])

    length = lengths[jnp.minimum(entry_mine, 5), lax.div(dp * 64 + sp, 8)]
    (
        project, attend, feed, turn_back, unfeed, feed_grads, unproject_out, unattend, qkv_grads, unproject,
    ) = encoder(
        length, w, carry, inputs, cot, act, igrad, hid, hid_sums, row_sums,
        mids, qkv, probs_even, probs_odd, invs, att, att_low, active, slope, low_a, low_b, dqkv, trans, trans_b, prm,
    )

    def run(layer, *steps):
        for of in range(LAYERS):
            chosen = [step for step in steps if step[0] == of]
            if chosen:

                @pl.when(layer == of)
                def _():
                    for _of, function, *arguments in chosen:
                        function(*arguments)

    def pairs(body, layer, hooks):
        def one(pair, carried):
            body(layer, pair)
            for at, of, function, *arguments in hooks:

                @pl.when(jnp.logical_and(pair == at, layer == of))
                def _():
                    function(*arguments)

            return carried

        lax.fori_loop(0, PAIRS, one, 0)

    def hidden_arrive():
        arrived(hid_all.at[1 - dp], b_send.at[0], b_recv.at[0])
        for side in range(2):
            for layer in range(LAYERS):
                hid[layer, :, side * (FF // 2) : (side + 1) * (FF // 2)] = hid_all[side, layer : layer + 1, :]

    slab_send(0)
    image_send(0)
    slab_send(1)
    slab_build_layer(1)
    hid_all[dp] = p_hid[...].astype(F32)
    push(hid_all.at[dp], hid_all.at[dp], b_send.at[0], b_recv.at[0], device(1 - dp, z, y, x, core))
    sent(gathers, lambda: hid_all.at[0], b_send, 0)
    onehot[...] = spread_matrix()
    invs[...] = jnp.zeros_like(invs)
    hid_sums[...] = jnp.zeros_like(hid_sums)
    row_sums[...] = jnp.zeros_like(row_sums)
    early[...] = jnp.zeros_like(early)
    slab_arrive(0)
    block_build(0)
    slab_send(2)
    slab_arrive(1)
    block_build(1)
    block_build(2)
    gather_direct(0)
    gather_z(1)
    slab_arrive(2)
    block_build(3)
    block_build(4)
    image_arrive(0)
    carry[...] = img[...].astype(F32)
    gather_z(2)
    gather_end(0)

    def forward(layer, carried):
        project(layer)
        run(layer, (0, gather_y, 1))
        pairs(
            attend,
            layer,
            ((0, 0, gather_z, 3), (0, 0, image_send, 1), (1, 0, gather_y, 2), (1, 1, gather_y, 4)),
        )
        run(
            layer,
            (0, gather_z, 4),
            (0, gather_y, 3),
            (0, hidden_arrive),
            (0, gather_end, 1),
            (0, gather_end, 2),
            (1, gather_end, 4),
        )
        feed(layer)
        run(layer, (0, gather_end, 3))
        return carried

    lax.fori_loop(0, LAYERS, forward, 0)
    back_send(0, 0, 8)
    image_arrive(1)
    turn_back()
    all_sent(gathers)

    def backward(step, carried):
        layer = LAYERS - 1 - step
        unfeed(layer)
        run(layer, (0, early_sum, 0), (0, reduce_z, 4), (0, reduce_y, 3))
        feed_grads(layer)
        run(layer, (0, reduce_core, 2))
        unproject_out(layer)
        run(
            layer,
            (1, reduce_core, 4),
            (0, reduce_core, 1),
            (0, early_sum, 1),
            (0, reduce_z, 3),
            (0, reduce_y, 2),
        )
        pairs(
            unattend,
            layer,
            (
                (0, 0, reduce_y, 1),
                (1, 0, early_sum, 2),
                (1, 0, reduce_slab, 4),
                (1, 0, reduce_z, 2),
                (1, 1, reduce_y, 4),
                (2, 0, reduce_z, 1),
            ),
        )
        run(layer, (0, reduce_slab, 3), (0, reduce_plane, 2), (0, early_sum, 3))
        qkv_grads(layer)
        run(layer, (1, reduce_core, 3), (0, reduce_core, 0))
        unproject(layer, lambda: run(layer, (0, back_send, 1, 0, 4), (0, reduce_direct, 0)))
        return carried

    lax.fori_loop(0, LAYERS, backward, 0)
    late_sum(0)
    back_send(1, 4, 8)
    early_sum(4)
    late_sum(1)
    reduce_end(2)
    reduce_slab(2)
    reduce_slab(1)
    reduce_plane(1)
    reduce_slab(0)
    reduce_plane(0)
    late_sum(2)
    reduce_end(1)
    for index in range(2):
        back_arrive(index)
    reduce_end(0)
    all_sent(reduces)


def finish_kernel(
    i_qkv, i_out, i_up, i_down, i_gains, i_biases, i_hid, i_act, i_igrad,
    act, igrad, g_qkv, g_out, g_up, g_down, g_gains, g_biases, g_hid,
):
    act[...] = i_act[...].astype(F32)
    igrad[...] = i_igrad[...].astype(F32)
    for source, target in (
        (i_qkv, g_qkv),
        (i_out, g_out),
        (i_up, g_up),
        (i_down, g_down),
        (i_gains, g_gains),
        (i_biases, g_biases),
        (i_hid, g_hid),
    ):
        target[...] = source[...]


def local(acts, cotangent, lengths, w_qkv, w_out, w_up, w_down, gains, biases, hidden_bias):
    swap = lambda array: array.transpose(1, 0, 2)
    vmem = pl.BlockSpec(memory_space=pltpu.VMEM)
    any_space = pl.BlockSpec(memory_space=pl.ANY)
    shape = jax.ShapeDtypeStruct
    buffer = pltpu.VMEM
    dma = pltpu.SemaphoreType.DMA
    pair = lambda *dims: [dma(dims), dma(dims)]
    results = pl.pallas_call(
        kernel,
        out_shape=(
            shape((3, LAYERS, 3 * D), F32),
            shape((3, LAYERS, D), F32),
            shape((3, LAYERS, FF), F32),
            shape((3, LAYERS, FF), F32),
            shape((LAYERS, 2, 3), F32),
            shape((3, LAYERS, 6), F32),
            shape((LAYERS, FF // 2), F32),
            shape((6, 96, D), BF),
            shape((6, 96, D), BF),
        ),
        in_specs=[pl.BlockSpec(memory_space=pltpu.SMEM), any_space, any_space] + [vmem] * 7,
        out_specs=(vmem,) * 7 + (any_space,) * 2,
        scratch_shapes=[
            buffer((LAYERS, D, WIDE), BF),
            buffer((TOK, D), F32),
            buffer((LAYERS, TOK, D), F32),
            buffer((TOK, D), BF),
            buffer((TOK, D), BF),
            buffer((TOK, D), BF),
            buffer((4 * ROWS, 256), BF),
            buffer((SLAB, 128), F32),
            buffer((2, LAYERS, FF // 2), F32),
            buffer((LAYERS, 1, FF), F32),
            buffer((LAYERS, 3, FC), F32),
            buffer((LAYERS, 8, D), F32),
            buffer((16, FC), F32),
            buffer((8, D), F32),
            buffer((D, 128), F32),
            *compute_scratch(),
            buffer((LAYERS, 2, SLAB, 128), BF),
            buffer((LAYERS, SPLIT, SLAB, 128), BF),
            buffer((LAYERS, SPLIT, SLAB, 128), BF),
            buffer((LAYERS, SPLIT, SLAB, 128), BF),
            buffer((16, FC), F32),
            buffer((16, FC), F32),
            buffer((3, 16, FC), F32),
            buffer((8, 16, FC), F32),
            buffer((3, 16, FC), F32),
            buffer((16, 8, D), F32),
            buffer((8, 8, D), F32),
            buffer((8, D), F32),
        ]
        + pair(len(GROUPS))
        + pair(COUNT)
        + pair(COUNT)
        + pair(COUNT)
        + [dma((2,)), dma((2,)), dma((2,)), dma((1,)), dma((1,))]
        + [dma((COUNT,)), dma((COUNT, 2))]
        + pair(COUNT)
        + pair(COUNT)
        + pair(len(GROUPS))
        + [dma((2,)), dma((2,)), dma((2,))]
        + pair(4)
        + pair(2)
        + [buffer((2, 4 * ROWS, unit[2]), BF) for unit in UNITS]
        + [buffer((4 * ROWS if index else 16, unit[2]), BF) for index, unit in enumerate(UNITS)]
        + [buffer((3 if index else 7, ROWS, unit[2]), BF) for index, unit in enumerate(UNITS)],
        compiler_params=pltpu.CompilerParams(
            collective_id=0, has_side_effects=True, vmem_limit_bytes=63 * MIB
        ),
        name="encoder",
    )(
        lengths, acts, cotangent, swap(w_qkv), swap(w_out), swap(w_up), swap(w_down),
        gains.transpose(0, 2, 1), swap(biases), hidden_bias,
    )
    act, igrad, g_qkv, g_out, g_up, g_down, g_gains, g_biases, g_hid = pl.pallas_call(
        finish_kernel,
        out_shape=(
            shape((6, 96, D), F32),
            shape((6, 96, D), F32),
            shape((3, LAYERS, 3 * D), F32),
            shape((3, LAYERS, D), F32),
            shape((3, LAYERS, FF), F32),
            shape((3, LAYERS, FF), F32),
            shape((LAYERS, 2, 3), F32),
            shape((3, LAYERS, 6), F32),
            shape((LAYERS, FF // 2), F32),
        ),
        in_specs=[vmem] * 9,
        out_specs=(vmem,) * 9,
        name="finish",
    )(*results)
    return (
        act,
        igrad,
        swap(g_qkv),
        swap(g_out),
        swap(g_up),
        swap(g_down),
        g_gains.transpose(0, 2, 1),
        swap(g_biases),
        g_hid,
    )


def solution(mesh):
    split = P(None, ("dp", "sp"), None)
    return jax.shard_map(
        local,
        mesh=mesh,
        in_specs=(split, split, P(), split, split, split, split, split, split, P(None, "dp")),
        out_specs=(split,) * 8 + (P(None, "dp"),),
        check_vma=False,
    )
```

time: 2370 us -> 136 us (0.06)
  blocking collectives: 1640 us -> 0 us
  waiting for transfers between devices: 269 us -> 0 us
  local copies, waits for them, and re-layouts: 161 us -> 0 us
  Pallas kernels: 0 us -> 135 us
  other arithmetic: 133 us -> 0 us
  matrix products: 125 us -> 0 us
    all_gather x9 -> x0, blocking collectives: 1570 us -> none  [the longest x2 441 us: fetch_layer(): lax.all_gather(w_out[layer_index], ('dp', 'sp'), axis=0, tiled=True)]
    ppermute x24 -> x0, waiting for transfers between devices: 181 us -> none  [swapped(): return lax.ppermute(block, axis, route)]
    pallas_call x0 -> x2, Pallas kernels: none -> 135 us  [the longest x1 133 us: local(): pl.pallas_call(kernel, out_shape=(shape((3, LAYERS, 3 * D), F32), shape((...]
    dot_general x36 -> x0, matrix products: 125 us -> none  [the longest x2 22.5 us: local(): jnp.einsum('mqhd,mkhd->mhqk', attended_grad, value_heads, preferred_eleme...]
    unnamed x6 -> x0, waiting for transfers between devices: 88.2 us -> none
    select_n x19 -> x0, other arithmetic: 74.2 us -> none  [the longest x10 40 us: collect_image(): jnp.where(upper_half, jnp.concatenate([other_value, value_part], 1), jnp....]
    unnamed x1 -> x0, blocking collectives: 65.6 us -> none
    unnamed x301 -> x0, local copies, waits for them, and re-layouts: 53.5 us -> none
  transfers between devices with their start and end apart: 29 -> 0, of which waited for: 13 -> 0; matrix products, arithmetic and copies ran while one was open for 12% -> 0% of each run, Pallas kernels for 0% -> 0%
where the time goes in v1:
time: 136 us
  Pallas kernels  135 us (99%)
    pallas_call x1, Pallas kernels, local(): pl.pallas_call(kernel, out_shape=(shape((3, LAYERS, 3 * D), F32), shape((...  133 us

profile of v1, /device:TPU:1, one launch (start us, length us, event | category | flops | bytes accessed | tf_op | source)
XLA Modules:
  0.0 136.2 jit_solution(18341133275272184280)
XLA Ops:
  0.6 132.9 %encoder.1 = (f32[3,2,1152]{2,1,0:T(2,128)}, f32[3,2,384]{2,1,0:T(2,128)}, f32[3,2,1536]{2,1,0:T(2,128)}, f32[3,2,1536]{2,1,0:T(2,128)}, f32[2,2,3]{2,1,0:T(2,12...) custom-call(s32[6,16]{1,0:T(8,128)} %lengths.1, ...), custom_call_target="tpu_custom_call" | custom-call | tf_op jit(solution)/shard_map/encoder/pallas_call | solution.py:1014
  133.5 2.6 %finish.1 = (f32[6,96,384]{2,1,0:T(8,128)}, f32[6,96,384]{2,1,0:T(8,128)}, f32[3,2,1152]{2,1,0:T(2,128)}, f32[3,2,384]{2,1,0:T(2,128)}, f32[3,2,1536]{2,1,0:T(2,...) custom-call(f32[3,2,1152]{2,1,0:T(2,128)} %get-tuple-element.27.i_qkv, ...), custom_call_target="tpu_custom_call" | custom-call | tf_op jit(solution)/shard_map/finish/pallas_call | solution.py:1082

commit v2 on v1

--- a/solution.py
+++ b/solution.py
@@ -88,9 +88,9 @@
     return jnp.sum(values.astype(F32), axis=0, keepdims=True)
 
 
-def each_block(body):
-    for start in range(0, TOK, RB):
-        body(slice(start, start + RB))
+def each_block(body, count=RB):
+    for start in range(0, TOK, count):
+        body(slice(start, start + count))
 
 
 def each_chunk(stop, width, body):
@@ -270,7 +270,7 @@
                 value_parts[which] += dot(trans[feature, rows], low)
             dqkv[rows, lane] = (jnp.where(first_half, results[0], results[1]) * scale).astype(BF)
 
-        each_block(body)
+        each_block(body, 768)
         dqkv[:, lanes_at(pair, D)] = jnp.concatenate(key_parts, axis=0).T.astype(BF)
         dqkv[:, lanes_at(pair, 2 * D)] = jnp.concatenate(value_parts, axis=0).T.astype(BF)
 

time: 136 us -> 137 us (level)
  no operation moved by 1% of the time
where the time goes in v2:
time: 137 us
  Pallas kernels  136 us (99%)
    pallas_call x1, Pallas kernels, local(): pl.pallas_call(kernel, out_shape=(shape((3, LAYERS, 3 * D), F32), shape((...  133 us

profile of v2, /device:TPU:1, one launch (start us, length us, event | category | flops | bytes accessed | tf_op | source)
XLA Modules:
  0.0 136.7 jit_solution(11218986222017017876)
XLA Ops:
  0.6 133.3 %encoder.1 = (f32[3,2,1152]{2,1,0:T(2,128)}, f32[3,2,384]{2,1,0:T(2,128)}, f32[3,2,1536]{2,1,0:T(2,128)}, f32[3,2,1536]{2,1,0:T(2,128)}, f32[2,2,3]{2,1,0:T(2,12...) custom-call(s32[6,16]{1,0:T(8,128)} %lengths.1, ...), custom_call_target="tpu_custom_call" | custom-call | tf_op jit(solution)/shard_map/encoder/pallas_call | solution.py:1014
  134.0 2.6 %finish.1 = (f32[6,96,384]{2,1,0:T(8,128)}, f32[6,96,384]{2,1,0:T(8,128)}, f32[3,2,1152]{2,1,0:T(2,128)}, f32[3,2,384]{2,1,0:T(2,128)}, f32[3,2,1536]{2,1,0:T(2,...) custom-call(f32[3,2,1152]{2,1,0:T(2,128)} %get-tuple-element.27.i_qkv, ...), custom_call_target="tpu_custom_call" | custom-call | tf_op jit(solution)/shard_map/finish/pallas_call | solution.py:1082

commit v3 on v1

--- a/solution.py
+++ b/solution.py
@@ -969,16 +969,16 @@
     lax.fori_loop(0, LAYERS, backward, 0)
     late_sum(0)
     back_send(1, 4, 8)
-    early_sum(4)
-    late_sum(1)
-    reduce_end(2)
     reduce_slab(2)
     reduce_slab(1)
     reduce_plane(1)
+    early_sum(4)
+    late_sum(1)
     reduce_slab(0)
     reduce_plane(0)
+    reduce_end(2)
+    reduce_end(1)
     late_sum(2)
-    reduce_end(1)
     for index in range(2):
         back_arrive(index)
     reduce_end(0)

time: 136 us -> 134 us (0.985)
  Pallas kernels: 135 us -> 133 us
    pallas_call x1, Pallas kernels: 133 us -> 130 us  [local(): pl.pallas_call(kernel, out_shape=(shape((3, LAYERS, 3 * D), F32), shape((...]
where the time goes in v3:
time: 134 us
  Pallas kernels  133 us (99%)
    pallas_call x1, Pallas kernels, local(): pl.pallas_call(kernel, out_shape=(shape((3, LAYERS, 3 * D), F32), shape((...  130 us

profile of v3, /device:TPU:1, one launch (start us, length us, event | category | flops | bytes accessed | tf_op | source)
XLA Modules:
  0.0 133.9 jit_solution(4521455891791496033)
XLA Ops:
  0.6 130.5 %encoder.1 = (f32[3,2,1152]{2,1,0:T(2,128)}, f32[3,2,384]{2,1,0:T(2,128)}, f32[3,2,1536]{2,1,0:T(2,128)}, f32[3,2,1536]{2,1,0:T(2,128)}, f32[2,2,3]{2,1,0:T(2,12...) custom-call(s32[6,16]{1,0:T(8,128)} %lengths.1, ...), custom_call_target="tpu_custom_call" | custom-call | tf_op jit(solution)/shard_map/encoder/pallas_call | solution.py:1014
  131.1 2.6 %finish.1 = (f32[6,96,384]{2,1,0:T(8,128)}, f32[6,96,384]{2,1,0:T(8,128)}, f32[3,2,1152]{2,1,0:T(2,128)}, f32[3,2,384]{2,1,0:T(2,128)}, f32[3,2,1536]{2,1,0:T(2,...) custom-call(f32[3,2,1152]{2,1,0:T(2,128)} %get-tuple-element.27.i_qkv, ...), custom_call_target="tpu_custom_call" | custom-call | tf_op jit(solution)/shard_map/finish/pallas_call | solution.py:1082
